TPU v7x, 32 devices: a whole 2x2x4 slice. The times are simulated.
32 devices in a mesh: groups: 2 (over x), wide: 16 (over z, y, core).
Axes of the slice: x: 2, y: 2, z: 4, core: 2. Of those that a mesh axis runs over, the one named last changes fastest.
Arguments:
- picture_feature_maps: bfloat16 [256, 10, 10, 1536], P(('groups', 'wide')), parts along dimension 0, may hold values from -6 to 6
- partitioned_filter_tensor: bfloat16 [3, 3, 128, 1536], replicated, may hold values from -0.1875 to 0.1875
- picture_token_layer_scaling: float32 [1536], replicated, may hold values from 0.1 to 1.9
- summary_probes: bfloat16 [64, 1536], replicated, may hold values from -6 to 6
- summary_probe_layer_scaling: float32 [1536], replicated, may hold values from 0.1 to 1.9
- asking_projection_tensor: bfloat16 [1536, 1536], P('wide'), may hold values from -0.15625 to 0.15625
- lookup_projection_tensor: bfloat16 [1536, 1536], P('wide'), may hold values from -0.15625 to 0.15625
- content_projection_tensor: bfloat16 [1536, 1536], P('wide'), may hold values from -0.15625 to 0.15625
- final_projection_tensor: bfloat16 [1536, 1536], P(None, 'wide'), may hold values from -0.15625 to 0.15625
- sharpness_coefficient: float32 [16], replicated, may hold values from 0.5 to 64
Outputs:
- attended: float32 [128, 1536], P('groups'), parts along dimension 0
- new_latents: bfloat16 [128, 1536], P('groups'), parts along dimension 0
There are 2 independent parts, one for each index of `groups`. A program takes and returns all parts, laid end to end along the dimension named above; an argument that names none is the same for every part. Nothing has to cross between parts.
All inputs are finite; a program needn't handle non-finite values.
Results may differ from a plain program's by a relative error of at most 0.004.
The roundings to bfloat16 on the way count: a program that leaves them out, or rounds other values in their place, can miss the bound.
Values may be sent and summed in bfloat16 or wider, within the bound.
A program may use at most 128 MiB of HBM per device.

v0:
```python
import math
import jax
import jax.numpy as jnp
from jax import lax
from jax.sharding import PartitionSpec as P

RESIDUAL_SCALE = 0.2
EPSILON = 1e-06


def layer_norm(values, gain):
    center = values - jnp.mean(values, axis=-1, keepdims=True)
    spread = jnp.mean(center * center, axis=-1, keepdims=True)
    return center * lax.rsqrt(spread + EPSILON) * gain


def combine(left_side, right_side):
    left_max, left_sum, left_weighted = left_side
    right_max, right_sum, right_weighted = right_side
    joint_max = jnp.maximum(left_max, right_max)
    scale_left = jnp.exp(left_max - joint_max)
    scale_right = jnp.exp(right_max - joint_max)
    return (
        joint_max,
        left_sum * scale_left + right_sum * scale_right,
        left_weighted * scale_left[..., None] + right_weighted * scale_right[..., None],
    )


def merge_all(row_max, row_sum, weighted):
    joint_max = lax.pmax(row_max, "wide")
    factor = jnp.exp(row_max - joint_max)
    joint_sum, joint_weighted = lax.psum((row_sum * factor, weighted * factor[..., None]), "wide")
    return (joint_max, joint_sum, joint_weighted)


def softmax_terms(scores, carried):
    row_max = jnp.max(scores, axis=-1)
    weights = jnp.exp(scores - row_max[..., None])
    row_sum = jnp.sum(weights, axis=-1)
    weighted = jnp.einsum("hlt,thd->hld", weights, carried, precision=lax.Precision.HIGHEST)
    return (row_max, row_sum, weighted)


def per_device(
    picture_feature_maps,
    partitioned_filter_tensor,
    picture_token_layer_scaling,
    summary_probes,
    summary_probe_layer_scaling,
    asking_projection_tensor,
    lookup_projection_tensor,
    content_projection_tensor,
    final_projection_tensor,
    sharpness_coefficient,
):
    channels = picture_feature_maps.shape[3]
    subspace_number_overall = sharpness_coefficient.shape[0]
    subspace_breadth = channels // subspace_number_overall
    lat_count = summary_probes.shape[0]
    activated = jax.nn.gelu(picture_feature_maps.astype(jnp.float32)).astype(jnp.bfloat16)
    convolved = lax.conv_general_dilated(
        activated,
        partitioned_filter_tensor,
        (1, 1),
        "SAME",
        dimension_numbers=("NHWC", "HWIO", "NHWC"),
        feature_group_count=channels // partitioned_filter_tensor.shape[2],
        preferred_element_type=jnp.float32,
    )
    summed = picture_feature_maps.astype(jnp.float32) + RESIDUAL_SCALE * convolved
    tok_norm = layer_norm(summed.reshape(-1, channels), picture_token_layer_scaling).astype(
        jnp.bfloat16
    )
    lat_norm = layer_norm(summary_probes.astype(jnp.float32), summary_probe_layer_scaling).astype(
        jnp.bfloat16
    )
    tok_count = tok_norm.shape[0]
    shard_rows = asking_projection_tensor.shape[0]
    first_row = lax.axis_index("wide") * shard_rows
    lat_slice = lax.dynamic_slice_in_dim(lat_norm, first_row, shard_rows, 1)
    probe_asking_vectors = lax.psum(
        jnp.dot(lat_slice, asking_projection_tensor, preferred_element_type=jnp.float32), "wide"
    )
    rescaled_similarity_logits = (
        probe_asking_vectors.reshape(lat_count, subspace_number_overall, subspace_breadth)
        * (sharpness_coefficient / math.sqrt(subspace_breadth))[None, :, None]
    )
    key_source = jnp.concatenate([tok_norm, lat_norm], axis=0)
    zero_rows = jnp.zeros((key_source.shape[0], channels), jnp.float32)

    def add_rows(running, weight_rows):
        return running + jnp.dot(key_source, weight_rows, preferred_element_type=jnp.float32)

    def scores_of(key_part):
        return jnp.einsum(
            "lhd,thd->hlt",
            rescaled_similarity_logits,
            key_part.reshape(-1, subspace_number_overall, subspace_breadth),
            precision=lax.Precision.HIGHEST,
        )

    running = (zero_rows, zero_rows)
    weight_rows = (
        lax.all_gather(lookup_projection_tensor, "wide", axis=0, tiled=True),
        lax.all_gather(content_projection_tensor, "wide", axis=0, tiled=True),
    )
    key_proj = add_rows(running[0], weight_rows[0])
    value_proj = add_rows(running[1], weight_rows[1])
    tok_terms = softmax_terms(
        scores_of(key_proj[:tok_count]),
        value_proj[:tok_count].reshape(-1, subspace_number_overall, subspace_breadth),
    )
    lat_terms = softmax_terms(
        scores_of(key_proj[tok_count:]),
        value_proj[tok_count:].reshape(-1, subspace_number_overall, subspace_breadth),
    )
    merged = merge_all(*tok_terms)
    joint_max, joint_sum, joint_weighted = combine(merged, lat_terms)
    attention = (
        (joint_weighted / joint_sum[..., None]).transpose(1, 0, 2).reshape(lat_count, channels)
    )
    attention_low = attention.astype(jnp.bfloat16)
    out_cols = jnp.dot(attention_low, final_projection_tensor, preferred_element_type=jnp.float32)
    attended = lax.all_gather(out_cols, "wide", axis=1, tiled=True)
    new_latents = (summary_probes.astype(jnp.float32) + attended).astype(jnp.bfloat16)
    return (attended, new_latents)


def solution(mesh):
    placed = (
        P(("groups", "wide"), None, None, None),
        P(),
        P(),
        P(),
        P(),
        P("wide", None),
        P("wide", None),
        P("wide", None),
        P(None, "wide"),
        P(),
    )
    return jax.shard_map(
        per_device,
        mesh=mesh,
        in_specs=placed,
        out_specs=(P("groups", None), P("groups", None)),
        check_vma=False,
    )
```

profile of v0, /device:TPU:0, one launch (start us, length us, event | category | flops | bytes accessed | tf_op | source)
XLA Modules:
  0.0 424.6 jit_solution(6361989302038620171)
XLA Ops:
  7.2 0.0 copy-start
  7.2 0.0 all-gather.4.cloned.1.call-start
  7.2 0.7 all-gather.4.cloned.1.call-update
  7.9 0.0 all-gather.6.cloned.1.call-start
  8.0 0.7 all-gather.6.cloned.1.call-update
  8.7 0.0 all-reduce.3.cloned.1.call-start
  8.7 1.1 convert_reduce_fusion
  9.8 1.2 fusion.34
  11.0 1.1 fusion.36
  12.0 0.0 copy-done
  12.0 0.3 fusion.41
  12.3 0.2 reshape.82
  12.5 1.0 copy.42
  13.5 0.0 all-reduce.3.cloned.1.call-update
  13.5 0.0 all-reduce.5.cloned.1.call-start
  13.5 6.2 %copy.43 = bf16[3,3,128,1536]{2,3,1,0:T(8,128)(2,1)} copy(bf16[3,3,128,1536]{3,2,1,0:T(8,128)(2,1)} %param.11) | data formatting | bytes 7077888 | tf_op args[1]
  19.7 0.0 copy-done.9
  19.7 9.5 %fusion.55 = (f32[8,10,10]{0,2,1:T(8,128)S(1)}, f32[8,10,10,1536]{3,0,2,1:T(8,128)}) fusion(bf16[3,3,128,12,128]{2,4,3,1,0:T(8,128)(2,1)} %bitcast.34, bf16[8,10,10,1536]{3,0,2,1:T(8,128)(2,1)S(1)} %copy-done.9), kind=kOutput, calls=%fused_computation.74 | convolution fusion | flops 2483453184 | bytes 10914944 | tf_op jit(solution)/shard_map/conv_general_dilated | solution.py:62
  29.2 0.1 copy.45
  29.3 0.1 copy.47
  29.5 0.0 slice-start.1
  29.5 8.7 %copy.44 = f32[8,10,10,1536]{3,2,1,0:T(8,128)} copy(f32[8,10,10,1536]{3,0,2,1:T(8,128)} %get-tuple-element.8) | data formatting | bytes 9830400 | tf_op jit(solution)/shard_map/add | solution.py:71
  38.2 0.0 slice-done
  38.2 0.6 multiply_reduce_fusion
  38.8 0.1 copy.48
  39.0 0.1 rsqrt.21
  39.1 0.0 copy-start.10
  39.1 0.0 copy-start.8
  39.1 6.6 %reshape.83 = f32[800,1536]{1,0:T(8,128)} reshape(f32[8,10,10,1536]{3,2,1,0:T(8,128)} %copy.44) | data formatting | bytes 9830400 | tf_op jit(solution)/shard_map/reshape | solution.py:72
  45.7 0.1 div.29
  45.9 0.0 copy-done.8
  45.9 3.1 multiply_convert_fusion
  49.0 17.4 %all-gather.4.cloned.1.call-done = bf16[1536,1536]{1,0:T(8,128)(2,1)} async-done(((bf16[96,1536]{1,0:T(8,128)(2,1)}), bf16[1536,1536]{1,0:T(8,128)(2,1)}) %all-gather.4.cloned.1.call-update) | async-done | bytes 4718608 | tf_op jit(solution)/shard_map/all_gather | solution.py:105
  66.4 8.6 %fusion.19 = f32[864,1536]{1,0:T(8,128)} fusion(bf16[1536,1536]{1,0:T(8,128)(2,1)} %all-gather.4.cloned.1.call-done, bf16[64,1536]{1,0:T(8,128)(2,1)S(1)} %fusion.36, bf16[800,1536]{1,0:T(8,128)(2,1)S(1)} %multiply_convert_fusion), kind=kOutput, calls=%fused_computation.25 | convolution fusion | flops 4082171904 | bytes 12681216 | tf_op jit(solution)/shard_map/dot_general | solution.py:93
  75.0 45.7 %all-gather.6.cloned.1.call-done = bf16[1536,1536]{1,0:T(8,128)(2,1)} async-done(((bf16[96,1536]{1,0:T(8,128)(2,1)}), bf16[1536,1536]{1,0:T(8,128)(2,1)}) %all-gather.6.cloned.1.call-update) | async-done | bytes 4718608 | tf_op jit(solution)/shard_map/all_gather | solution.py:106
  120.7 6.5 %fusion.18 = f32[864,1536]{1,0:T(8,128)S(1)} fusion(bf16[1536,1536]{1,0:T(8,128)(2,1)} %all-gather.6.cloned.1.call-done, bf16[64,1536]{1,0:T(8,128)(2,1)S(1)} %fusion.36, bf16[800,1536]{1,0:T(8,128)(2,1)S(1)} %multiply_convert_fusion), kind=kOutput, calls=%fused_computation.24 | convolution fusion | flops 4082171904 | bytes 12681216 | tf_op jit(solution)/shard_map/dot_general | solution.py:93
  127.2 2.8 slice.16
  130.0 2.5 slice.17
  132.5 6.0 %copy.50 = f32[800,1536]{0,1:T(8,128)} copy(f32[800,1536]{1,0:T(8,128)} %slice.16) | data formatting | bytes 9830400 | tf_op jit(solution)/shard_map/slice | solution.py:111
  138.5 74.2 %all-reduce.3.cloned.1.call-done = f32[64,16,96]{2,0,1:T(8,128)} async-done(((f32[64,16,96]{2,0,1:T(8,128)}), f32[64,16,96]{2,0,1:T(8,128)}) %all-reduce.3.cloned.1.call-update) | async-done | bytes 393232 | tf_op jit(solution)/shard_map/psum | solution.py:82
  212.7 8.3 %fusion.56 = (f32[16,64]{1,0:T(8,128)S(1)}, f32[16,64,800]{2,1,0:T(8,128)}) fusion(f32[800,16,96]{0,2,1:T(8,128)} %bitcast.30, f32[64,16,96]{2,0,1:T(8,128)} %all-reduce.3.cloned.1.call-done, f32[16]{0:T(128)S(1)} %broadcast_multiply_fusion.1), kind=kOutput, calls=%fused_computation.75 | convolution fusion | flops 944634880 | bytes 8589376 | tf_op jit(solution)/shard_map/lhd,thd->hlt/dot_general | solution.py:96
  221.0 32.4 %pmax.7 = f32[16,64]{1,0:T(8,128)S(1)} all-reduce(f32[16,64]{1,0:T(8,128)S(1)} %get-tuple-element.9), channel_id=1, replica_groups=mesh['groups'=2,'wide'=16] {'wide'}, use_global_device_ids=true, to_apply=%region_6.0 | all-reduce | flops 1024 | bytes 8192 | tf_op jit(solution)/shard_map/pmax | solution.py:31
  253.5 2.9 fusion.6
  256.4 30.0 %psum.23 = f32[16,64]{1,0:T(8,128)S(1)} all-reduce(f32[16,64]{1,0:T(8,128)S(1)} %get-tuple-element.5), channel_id=1, replica_groups=mesh['groups'=2,'wide'=16] {'wide'}, use_global_device_ids=true, to_apply=%region_10.0 | all-reduce | flops 1024 | bytes 8192 | tf_op jit(solution)/shard_map/psum | solution.py:33
  286.4 0.2 reshape.86
  286.6 6.0 %copy.51 = f32[800,1536]{0,1:T(8,128)} copy(f32[800,1536]{1,0:T(8,128)} %slice.17) | data formatting | bytes 9830400 | tf_op jit(solution)/shard_map/slice | solution.py:112
  292.6 11.3 %fusion.20 = f32[16,64,96]{2,1,0:T(8,128)} fusion(f32[800,16,96]{0,2,1:T(8,128)} %bitcast.31, f32[16,64,800]{2,1,0:T(8,128)} %get-tuple-element.10, f32[16,64]{1,0:T(8,128)S(1)} %get-tuple-element.9, f32[16,64]{1,0:T(8,128)S(1)} %get-tuple-element.6), kind=kOutput, calls=%fused_computation.26 | convolution fusion | flops 944635904 | bytes 8593408 | tf_op jit(solution)/shard_map/hlt,thd->hld/dot_general | solution.py:41
  303.8 0.0 all-reduce.5.cloned.1.call-update
  303.9 0.0 copy-start.4
  303.9 0.0 copy-start.1
  303.9 0.2 reshape.87
  304.1 1.1 fusion.57
  305.2 0.1 fusion.33
  305.4 85.9 %all-reduce.5.cloned.1.call-done = f32[16,64,96]{2,1,0:T(8,128)} async-done(((f32[16,64,96]{2,1,0:T(8,128)}), f32[16,64,96]{2,1,0:T(8,128)}) %all-reduce.5.cloned.1.call-update) | async-done | bytes 393232 | tf_op jit(solution)/shard_map/psum | solution.py:33
  391.3 2.5 fusion.24
  393.8 0.2 copy.55
  393.9 0.3 convert_element_type.39
  394.2 0.2 convolution_bitcast_fusion
  394.4 22.2 %all-gather = f32[16,96,64]{1,2,0:T(8,128)S(1)} all-gather(f32[1,96,64]{1,2,0:T(8,128)S(1)} %convolution_bitcast_fusion), channel_id=1, replica_groups=mesh['groups'=2,'wide'=16] {'wide'}, dimensions={0}, use_global_device_ids=true | all-gather | bytes 417792 | tf_op jit(solution)/shard_map/all_gather | solution.py:125
  416.7 0.3 copy.56
  417.0 0.2 reshape.89
  417.2 0.0 copy-start.6
  417.2 0.8 fusion.37
  418.0 0.0 copy-done.6
  (28 shorter events, 0.1 us)
Async XLA Ops:
  7.2 4.9 %copy-start = (bf16[96,1536]{1,0:T(8,128)(2,1)S(1)}, bf16[96,1536]{1,0:T(8,128)(2,1)}, u32[]{:S(2)}) copy-start(bf16[96,1536]{1,0:T(8,128)(2,1)} %param.15) | copy-start | bytes 884740
  7.2 59.2 %all-gather.4.cloned.1.call-start = ((), (), s32[]{:S(2)}) async-start(), calls=%async_computation.1 | async-start | bytes 5013504 | tf_op jit(solution)/shard_map/all_gather | solution.py:105
  7.9 112.8 %all-gather.6.cloned.1.call-start = ((), (), s32[]{:S(2)}) async-start(), calls=%async_computation.2 | async-start | bytes 5013504 | tf_op jit(solution)/shard_map/all_gather | solution.py:106
  8.7 204.1 %all-reduce.3.cloned.1.call-start = ((), (), s32[]{:S(2)}) async-start(), calls=%async_computation | async-start | bytes 1048576 | tf_op jit(solution)/shard_map/psum | solution.py:82
  13.5 6.3 %copy-start.9 = (bf16[8,10,10,1536]{3,0,2,1:T(8,128)(2,1)S(1)}, bf16[8,10,10,1536]{3,0,2,1:T(8,128)(2,1)}, u32[]{:S(2)}) copy-start(bf16[8,10,10,1536]{3,0,2,1:T(8,128)(2,1)} %param.10) | copy-start | bytes 7372804
  13.5 377.8 %all-reduce.5.cloned.1.call-start = ((), (), s32[]{:S(2)}) async-start(), calls=%async_computation.3 | async-start | bytes 1048576 | tf_op jit(solution)/shard_map/psum | solution.py:33
  29.3 8.8 %slice-start = ((s8[4915200]{0:T(1024)(128)(4,1)}), s8[720896]{0:T(1024)(128)(4,1)S(1)}, s32[]{:S(2)}) async-start(s8[4915200]{0:T(1024)(128)(4,1)} %bitcast.32), calls=%async_computation.4 | async-start | bytes 1441792
  29.5 8.7 %slice-start.1 = ((s8[4915200]{0:T(1024)(128)(4,1)}), s8[4194304]{0:T(1024)(128)(4,1)S(1)}, s32[]{:S(2)}) async-start(s8[4915200]{0:T(1024)(128)(4,1)} %bitcast.32), calls=%async_computation.5 | async-start | bytes 8388608
  39.1 6.8 %copy-start.10 = (f32[16]{0:T(128)S(1)}, f32[16]{0:T(128)}, u32[]{:S(2)}) copy-start(f32[16]{0:T(128)} %param.19) | copy-start | bytes 196
  39.1 6.8 %copy-start.8 = (f32[1536]{0:T(1024)S(1)}, f32[1536]{0:T(1024)}, u32[]{:S(2)}) copy-start(f32[1536]{0:T(1024)} %param.12) | copy-start | bytes 18436
  120.7 6.5 %copy-start.2 = (f32[864,1536]{1,0:T(8,128)S(1)}, f32[864,1536]{1,0:T(8,128)}, u32[]{:S(2)}) copy-start(f32[864,1536]{1,0:T(8,128)} %fusion.19) | copy-start | bytes 15925252
  127.2 5.4 %copy-start.3 = (f32[864,1536]{1,0:T(8,128)}, f32[864,1536]{1,0:T(8,128)S(1)}, u32[]{:S(2)}) copy-start(f32[864,1536]{1,0:T(8,128)S(1)} %fusion.18) | copy-start | bytes 15925252
  212.7 73.7 %slice-start.2 = ((f32[864,1536]{1,0:T(8,128)}), f32[64,1536]{1,0:T(8,128)S(1)}, s32[]{:S(2)}) async-start(f32[864,1536]{1,0:T(8,128)} %fusion.19), calls=%async_computation.6 | async-start | bytes 786432 | tf_op jit(solution)/shard_map/slice | solution.py:115
  292.5 11.3 %slice-start.3 = ((f32[864,1536]{1,0:T(8,128)}), f32[64,1536]{1,0:T(8,128)S(1)}, s32[]{:S(2)}) async-start(f32[864,1536]{1,0:T(8,128)} %copy-done.3), calls=%async_computation.7 | async-start | bytes 786432 | tf_op jit(solution)/shard_map/slice | solution.py:116
  292.6 11.5 %copy-start.5 = (f32[64,16,96]{2,0,1:T(8,128)S(1)}, f32[64,16,96]{2,0,1:T(8,128)}, u32[]{:S(2)}) copy-start(f32[64,16,96]{2,0,1:T(8,128)} %all-reduce.3.cloned.1.call-done) | copy-start | bytes 1179652
  303.8 90.4 %copy-start.7 = (bf16[1536,96]{0,1:T(8,128)(2,1)S(1)}, bf16[1536,96]{0,1:T(8,128)(2,1)}, u32[]{:S(2)}) copy-start(bf16[1536,96]{0,1:T(8,128)(2,1)} %param.18) | copy-start | bytes 884740
  303.9 113.4 %copy-start.4 = (bf16[64,1536]{1,0:T(8,128)(2,1)S(1)}, bf16[64,1536]{1,0:T(8,128)(2,1)}, u32[]{:S(2)}) copy-start(bf16[64,1536]{1,0:T(8,128)(2,1)} %param.13) | copy-start | bytes 589828
  303.9 114.2 %copy-start.1 = (bf16[96,1536]{1,0:T(8,128)(2,1)S(1)}, bf16[96,1536]{1,0:T(8,128)(2,1)}, u32[]{:S(2)}) copy-start(bf16[96,1536]{1,0:T(8,128)(2,1)} %param.15) | copy-start | bytes 884740
  417.2 0.8 copy-start.6
Sparse Core Ops, SparseCore 0:
  10.3 56.0 all-gather.3
  68.7 51.9 all-gather.5
  124.1 88.5 all-reduce.2
  304.0 87.2 all-reduce.4
where the time goes:
time: 425 us
  waiting for transfers between devices  225 us (53%)
  blocking collectives  84.7 us (20%)
  matrix products  48.2 us (11%)
  local copies, waits for them, and re-layouts  42 us (10%)
  between operations  14.1 us (3%)
  other arithmetic  10.9 us (3%)
    psum x1, waiting for transfers between devices, merge_all(): lax.psum((row_sum * factor, weighted * factor[..., None]), 'wide')  85.9 us
    psum x1, waiting for transfers between devices, per_device(): lax.psum(jnp.dot(lat_slice, asking_projection_tensor, preferred_element_t...  74.2 us
    all_gather x1, waiting for transfers between devices, per_device(): lax.all_gather(content_projection_tensor, 'wide', axis=0, tiled=True)  45.7 us
    pmax x1, blocking collectives, merge_all(): joint_max = lax.pmax(row_max, 'wide')  32.4 us
    psum x1, blocking collectives, merge_all(): lax.psum((row_sum * factor, weighted * factor[..., None]), 'wide')  30 us
    all_gather x1, blocking collectives, per_device(): attended = lax.all_gather(out_cols, 'wide', axis=1, tiled=True)  22.2 us
    all_gather x1, waiting for transfers between devices, per_device(): lax.all_gather(lookup_projection_tensor, 'wide', axis=0, tiled=True)  17.4 us
    dot_general x2, matrix products, add_rows(): jnp.dot(key_source, weight_rows, preferred_element_type=jnp.float32)  15 us
  transfers between devices with their start and end apart: 4, of which 4 were waited for; matrix products, arithmetic and copies ran while one was open for 16% of the time, Pallas kernels for 0%

commit v1 on v0

--- a/solution.py
+++ b/solution.py
@@ -6,6 +6,19 @@
 
 RESIDUAL_SCALE = 0.2
 EPSILON = 1e-06
+
+
+def collect(array, axis, dim):
+    ways = lax.axis_size(axis)
+    up = [(d, (d + 1) % ways) for d in range(ways)]
+    down = [(d, (d - 1) % ways) for d in range(ways)]
+    earlier, later = ([array], [array])
+    for _ in range(ways // 2):
+        earlier.append(lax.ppermute(earlier[-1], axis, up))
+    for _ in range((ways - 1) // 2):
+        later.append(lax.ppermute(later[-1], axis, down))
+    line = jnp.concatenate([*earlier[::-1], *later[1:]], axis=dim)
+    return jnp.roll(line, (lax.axis_index(axis) - ways // 2) * array.shape[dim], axis=dim)
 
 
 def layer_norm(values, gain):
@@ -102,7 +115,7 @@
 
     running = (zero_rows, zero_rows)
     weight_rows = (
-        lax.all_gather(lookup_projection_tensor, "wide", axis=0, tiled=True),
+        collect(lookup_projection_tensor, "wide", 0),
         lax.all_gather(content_projection_tensor, "wide", axis=0, tiled=True),
     )
     key_proj = add_rows(running[0], weight_rows[0])

time: 425 us -> 370 us (0.87)
  waiting for transfers between devices: 225 us -> 113 us
  starting transfers between devices: 0.16 us -> 32.4 us
  local copies, waits for them, and re-layouts: 42 us -> 62.4 us
    psum x1, waiting for transfers between devices: 74.2 us -> 5.61 us  [per_device(): lax.psum(jnp.dot(lat_slice, asking_projection_tensor, preferred_element_t...]
    all_gather x1, waiting for transfers between devices: 45.7 us -> 0.02 us  [per_device(): lax.all_gather(content_projection_tensor, 'wide', axis=0, tiled=True)]
    ppermute x0 -> x15, starting transfers between devices: none -> 32.3 us  [the longest x7 31.7 us: collect(): later.append(lax.ppermute(later[-1], axis, down))]
    ppermute x0 -> x15, waiting for transfers between devices: none -> 19.6 us  [the longest x8 19.1 us: collect(): earlier.append(lax.ppermute(earlier[-1], axis, up))]
    unnamed x28 -> x87, local copies, waits for them, and re-layouts: 6.53 us -> 25.6 us
    all_gather x1 -> x0, waiting for transfers between devices: 17.4 us -> none  [per_device(): lax.all_gather(lookup_projection_tensor, 'wide', axis=0, tiled=True)]
    dot_general x2, matrix products: 15 us -> 10.5 us  [add_rows(): jnp.dot(key_source, weight_rows, preferred_element_type=jnp.float32)]
  transfers between devices with their start and end apart: 4 -> 18, of which waited for: 4 -> 8; matrix products, arithmetic and copies ran while one was open for 16% -> 24% of each run, Pallas kernels for 0% -> 0%
where the time goes in v1:
time: 370 us; the launch traced here: 369 us
  waiting for transfers between devices  113 us (31%)
  blocking collectives  85.9 us (23%)
  local copies, waits for them, and re-layouts  62.4 us (17%)
  matrix products  45.9 us (12%)
  starting transfers between devices  32.4 us (9%)
  between operations  14.5 us (4%)
  other arithmetic  14.4 us (4%)
    psum x1, waiting for transfers between devices, merge_all(): lax.psum((row_sum * factor, weighted * factor[..., None]), 'wide')  87.2 us
    pmax x1, blocking collectives, merge_all(): joint_max = lax.pmax(row_max, 'wide')  33.2 us
    ppermute x7, starting transfers between devices, collect(): later.append(lax.ppermute(later[-1], axis, down))  31.7 us
    psum x1, blocking collectives, merge_all(): lax.psum((row_sum * factor, weighted * factor[..., None]), 'wide')  30.4 us
    unnamed x87, local copies, waits for them, and re-layouts  25.6 us
    all_gather x1, blocking collectives, per_device(): attended = lax.all_gather(out_cols, 'wide', axis=1, tiled=True)  22.2 us
    ppermute x8, waiting for transfers between devices, collect(): earlier.append(lax.ppermute(earlier[-1], axis, up))  19.1 us
    dot_general x2, matrix products, softmax_terms(): jnp.einsum('hlt,thd->hld', weights, carried, precision=lax.Precision.HIGH...  13.7 us
  transfers between devices with their start and end apart: 18, of which 8 were waited for; matrix products, arithmetic and copies ran while one was open for 24% of the time, Pallas kernels for 0%

profile of v1, /device:TPU:0, one launch (start us, length us, event | category | flops | bytes accessed | tf_op | source)
XLA Modules:
  0.0 368.7 jit_solution(5779345344132242396)
XLA Ops:
  7.2 0.5 collective-permute-start
  7.7 5.1 %collective-permute-start.8 = (bf16[96,1536]{1,0:T(8,128)(2,1)}, bf16[96,1536]{1,0:T(8,128)(2,1)S(1)}, u32[]{:S(2)}, u32[]{:S(2)}) collective-permute-start(bf16[96,1536]{1,0:T(8,128)(2,1)} %param.16), channel_id=1, source_target_pairs={{0,15},{1,0},{2,1},{3,2},{4,3},{5,4},{6,5},{7,6},{8,7},{9,8},{10,9... | collective-permute-start | bytes 884744 | tf_op jit(solution)/shard_map/ppermute | solution.py:19
  12.8 4.7 %collective-permute-done = bf16[96,1536]{1,0:T(8,128)(2,1)S(1)} collective-permute-done((bf16[96,1536]{1,0:T(8,128)(2,1)}, bf16[96,1536]{1,0:T(8,128)(2,1)S(1)}, u32[]{:S(2)}, u32[]{:S(2)}) %collective-permute-start) | collective-permute-done | bytes 294944 | tf_op jit(solution)/shard_map/ppermute | solution.py:17
  17.5 1.1 convert_reduce_fusion
  18.6 7.7 %collective-permute-done.1 = bf16[96,1536]{1,0:T(8,128)(2,1)S(1)} collective-permute-done((bf16[96,1536]{1,0:T(8,128)(2,1)S(1)}, bf16[96,1536]{1,0:T(8,128)(2,1)S(1)}, u32[]{:S(2)}, u32[]{:S(2)}) %collective-permute-start.1) | collective-permute-done | bytes 294944 | tf_op jit(solution)/shard_map/ppermute | solution.py:17
  26.3 1.3 fusion.35
  27.6 4.4 %collective-permute-start.9 = (bf16[96,1536]{1,0:T(8,128)(2,1)S(1)}, bf16[96,1536]{1,0:T(8,128)(2,1)S(1)}, u32[]{:S(2)}, u32[]{:S(2)}) collective-permute-start(bf16[96,1536]{1,0:T(8,128)(2,1)S(1)} %collective-permute-done.8), channel_id=1, source_target_pairs={{0,15},{1,0},{2,1},{3,2},{4,3},{5,4},{6,5},{7,6},{8,7},{9,8},{10,9... | collective-permute-start | bytes 884744 | tf_op jit(solution)/shard_map/ppermute | solution.py:19
  32.0 3.3 collective-permute-done.2
  35.3 1.2 fusion.37
  36.5 4.5 %collective-permute-start.10 = (bf16[96,1536]{1,0:T(8,128)(2,1)S(1)}, bf16[96,1536]{1,0:T(8,128)(2,1)S(1)}, u32[]{:S(2)}, u32[]{:S(2)}) collective-permute-start(bf16[96,1536]{1,0:T(8,128)(2,1)S(1)} %collective-permute-done.9), channel_id=1, source_target_pairs={{0,15},{1,0},{2,1},{3,2},{4,3},{5,4},{6,5},{7,6},{8,7},{9,8},{10,9... | collective-permute-start | bytes 884744 | tf_op jit(solution)/shard_map/ppermute | solution.py:19
  40.9 3.3 collective-permute-done.3
  44.2 0.3 fusion.42
  44.7 1.0 copy.42
  45.7 0.7 all-gather.3.cloned.1.call-update
  46.5 6.0 %copy.43 = bf16[3,3,128,1536]{2,3,1,0:T(8,128)(2,1)} copy(bf16[3,3,128,1536]{3,2,1,0:T(8,128)(2,1)} %param.11) | data formatting | bytes 7077888 | tf_op args[1]
  52.5 4.4 %collective-permute-start.11 = (bf16[96,1536]{1,0:T(8,128)(2,1)S(1)}, bf16[96,1536]{1,0:T(8,128)(2,1)S(1)}, u32[]{:S(2)}, u32[]{:S(2)}) collective-permute-start(bf16[96,1536]{1,0:T(8,128)(2,1)S(1)} %collective-permute-done.10), channel_id=1, source_target_pairs={{0,15},{1,0},{2,1},{3,2},{4,3},{5,4},{6,5},{7,6},{8,7},{9,8},{10,9... | collective-permute-start | bytes 884744 | tf_op jit(solution)/shard_map/ppermute | solution.py:19
  56.9 10.8 %fusion.57 = (f32[8,10,10]{0,2,1:T(8,128)S(1)}, f32[8,10,10,1536]{3,0,2,1:T(8,128)}) fusion(bf16[3,3,128,12,128]{2,4,3,1,0:T(8,128)(2,1)} %bitcast.31, bf16[8,10,10,1536]{3,0,2,1:T(8,128)(2,1)} %param.10), kind=kOutput, calls=%fused_computation.108 | convolution fusion | flops 2483453184 | bytes 10914944 | tf_op jit(solution)/shard_map/conv_general_dilated | solution.py:75
  68.0 4.4 %collective-permute-start.12 = (bf16[96,1536]{1,0:T(8,128)(2,1)S(1)}, bf16[96,1536]{1,0:T(8,128)(2,1)}, u32[]{:S(2)}, u32[]{:S(2)}) collective-permute-start(bf16[96,1536]{1,0:T(8,128)(2,1)S(1)} %collective-permute-done.11), channel_id=1, source_target_pairs={{0,15},{1,0},{2,1},{3,2},{4,3},{5,4},{6,5},{7,6},{8,7},{9,8},{10,9... | collective-permute-start | bytes 884744 | tf_op jit(solution)/shard_map/ppermute | solution.py:19
  72.5 3.2 multiply_reduce_fusion
  75.6 8.5 %copy.44 = f32[8,10,10,1536]{3,2,1,0:T(8,128)} copy(f32[8,10,10,1536]{3,0,2,1:T(8,128)} %get-tuple-element.8) | data formatting | bytes 9830400 | tf_op jit(solution)/shard_map/add | solution.py:84
  84.4 7.3 %reshape.83 = f32[800,1536]{1,0:T(8,128)} reshape(f32[8,10,10,1536]{3,2,1,0:T(8,128)} %copy.44) | data formatting | bytes 9830400 | tf_op jit(solution)/shard_map/reshape | solution.py:85
  91.9 4.3 %collective-permute-start.13 = (bf16[96,1536]{1,0:T(8,128)(2,1)}, bf16[96,1536]{1,0:T(8,128)(2,1)}, u32[]{:S(2)}, u32[]{:S(2)}) collective-permute-start(bf16[96,1536]{1,0:T(8,128)(2,1)} %collective-permute-done.12), channel_id=1, source_target_pairs={{0,15},{1,0},{2,1},{3,2},{4,3},{5,4},{6,5},{7,6},{8,7},{9,8},{10,9... | collective-permute-start | bytes 884744 | tf_op jit(solution)/shard_map/ppermute | solution.py:19
  96.2 3.1 multiply_convert_fusion
  99.4 0.8 broadcast_multiply_fusion.1
  100.2 0.5 collective-permute-done.13
  100.8 4.6 %collective-permute-start.14 = (bf16[96,1536]{1,0:T(8,128)(2,1)}, bf16[96,1536]{1,0:T(8,128)(2,1)S(1)}, u32[]{:S(2)}, u32[]{:S(2)}) collective-permute-start(bf16[96,1536]{1,0:T(8,128)(2,1)} %collective-permute-done.13), channel_id=1, source_target_pairs={{0,15},{1,0},{2,1},{3,2},{4,3},{5,4},{6,5},{7,6},{8,7},{9,8},{10,9... | collective-permute-start | bytes 884744 | tf_op jit(solution)/shard_map/ppermute | solution.py:19
  105.5 1.0 constant_dynamic-update-slice_fusion.31
  106.5 1.0 constant_dynamic-update-slice_fusion.30
  107.5 1.0 constant_dynamic-update-slice_fusion.29
  108.5 1.0 constant_dynamic-update-slice_fusion.28
  109.5 1.0 constant_dynamic-update-slice_fusion.27
  110.5 1.0 constant_dynamic-update-slice_fusion.26
  111.5 1.0 constant_dynamic-update-slice_fusion.25
  112.5 1.0 constant_dynamic-update-slice_fusion.21
  113.5 1.0 constant_dynamic-update-slice_fusion.20
  114.5 1.0 constant_dynamic-update-slice_fusion.19
  115.5 1.0 constant_dynamic-update-slice_fusion.18
  116.5 1.0 constant_dynamic-update-slice_fusion.17
  117.5 1.0 constant_dynamic-update-slice_fusion.15
  118.5 1.0 constant_dynamic-update-slice_fusion.14
  119.9 1.0 constant_dynamic-update-slice_fusion.2
  120.9 1.0 constant_dynamic-update-slice_fusion.1
  121.9 4.3 %fusion.6 = f32[864,1536]{1,0:T(8,128)S(1)} fusion(bf16[3072,1536]{1,0:T(8,128)(2,1)S(1)} %constant_dynamic-update-slice_fusion, s32[]{:T(128)S(6)} %select_n.18, bf16[64,1536]{1,0:T(8,128)(2,1)S(1)} %fusion.37, bf16[800,1536]{1,0:T(8,128)(2,1)S(1)} %multiply_convert_fusion), kind=kOutput, calls=%fused_computation.13 | convolution fusion | flops 4082171904 | bytes 12681220 | tf_op jit(solution)/shard_map/dot_general | solution.py:106
  126.3 2.6 slice.16
  128.9 1.0 reshape.86
  129.8 6.0 %copy.50 = f32[800,1536]{0,1:T(8,128)} copy(f32[800,1536]{1,0:T(8,128)} %slice.16) | data formatting | bytes 9830400 | tf_op jit(solution)/shard_map/slice | solution.py:124
  135.8 5.6 %all-reduce.3.cloned.1.call-done = f32[64,16,96]{2,0,1:T(8,128)} async-done(((f32[64,16,96]{2,0,1:T(8,128)}), f32[64,16,96]{2,0,1:T(8,128)}) %all-reduce.3.cloned.1.call-update) | async-done | bytes 393232 | tf_op jit(solution)/shard_map/psum | solution.py:95
  141.5 8.3 %fusion.58 = (f32[16,64]{1,0:T(8,128)S(1)}, f32[16,64,800]{2,1,0:T(8,128)}) fusion(f32[800,16,96]{0,2,1:T(8,128)} %bitcast.29, f32[64,16,96]{2,0,1:T(8,128)} %all-reduce.3.cloned.1.call-done, f32[16]{0:T(128)S(1)} %broadcast_multiply_fusion.1), kind=kOutput, calls=%fused_computation.109 | convolution fusion | flops 944634880 | bytes 8589376 | tf_op jit(solution)/shard_map/lhd,thd->hlt/dot_general | solution.py:109
  149.8 33.2 %pmax.7 = f32[16,64]{1,0:T(8,128)S(1)} all-reduce(f32[16,64]{1,0:T(8,128)S(1)} %get-tuple-element.9), channel_id=1, replica_groups=mesh['groups'=2,'wide'=16] {'wide'}, use_global_device_ids=true, to_apply=%region_6.7 | all-reduce | flops 1024 | bytes 8192 | tf_op jit(solution)/shard_map/pmax | solution.py:44
  183.0 2.9 fusion.8
  185.9 30.4 %psum.23 = f32[16,64]{1,0:T(8,128)S(1)} all-reduce(f32[16,64]{1,0:T(8,128)S(1)} %get-tuple-element.5), channel_id=1, replica_groups=mesh['groups'=2,'wide'=16] {'wide'}, use_global_device_ids=true, to_apply=%region_10.11 | all-reduce | flops 1024 | bytes 8192 | tf_op jit(solution)/shard_map/psum | solution.py:46
  216.3 2.2 fusion.59
  218.5 0.8 copy-done.5
  219.5 6.1 %fusion.20 = f32[864,1536]{1,0:T(8,128)S(1)} fusion(bf16[1536,1536]{1,0:T(8,128)(2,1)} %all-gather.3.cloned.1.call-done, bf16[64,1536]{1,0:T(8,128)(2,1)S(1)} %fusion.37, bf16[800,1536]{1,0:T(8,128)(2,1)S(1)} %multiply_convert_fusion), kind=kOutput, calls=%fused_computation.26 | convolution fusion | flops 4082171904 | bytes 12681216 | tf_op jit(solution)/shard_map/dot_general | solution.py:106
  225.6 2.4 copy-done.2
  228.0 2.6 slice.17
  230.6 6.1 %copy.51 = f32[800,1536]{0,1:T(8,128)} copy(f32[800,1536]{1,0:T(8,128)} %slice.17) | data formatting | bytes 9830400 | tf_op jit(solution)/shard_map/slice | solution.py:125
  236.7 11.3 %fusion.21 = f32[16,64,96]{2,1,0:T(8,128)} fusion(f32[800,16,96]{0,2,1:T(8,128)} %bitcast.30, f32[16,64,800]{2,1,0:T(8,128)} %get-tuple-element.10, f32[16,64]{1,0:T(8,128)S(1)} %get-tuple-element.9, f32[16,64]{1,0:T(8,128)S(1)} %get-tuple-element.6), kind=kOutput, calls=%fused_computation.27 | convolution fusion | flops 944635904 | bytes 8593408 | tf_op jit(solution)/shard_map/hlt,thd->hld/dot_general | solution.py:54
  248.2 87.2 %all-reduce.5.cloned.1.call-done = f32[16,64,96]{2,1,0:T(8,128)} async-done(((f32[16,64,96]{2,1,0:T(8,128)}), f32[16,64,96]{2,1,0:T(8,128)}) %all-reduce.5.cloned.1.call-update) | async-done | bytes 393232 | tf_op jit(solution)/shard_map/psum | solution.py:46
  335.4 2.5 fusion.25
  338.1 0.3 convert_element_type.39
  338.6 22.2 %all-gather = f32[16,96,64]{1,2,0:T(8,128)S(1)} all-gather(f32[1,96,64]{1,2,0:T(8,128)S(1)} %convolution_bitcast_fusion), channel_id=1, replica_groups=mesh['groups'=2,'wide'=16] {'wide'}, dimensions={0}, use_global_device_ids=true | all-gather | bytes 417792 | tf_op jit(solution)/shard_map/all_gather | solution.py:138
  360.8 0.3 copy.56
  361.4 0.8 fusion.38
  (113 shorter events, 2.7 us)
Async XLA Ops:
  7.2 37.1 %copy-start = (bf16[96,1536]{1,0:T(8,128)(2,1)S(1)}, bf16[96,1536]{1,0:T(8,128)(2,1)}, u32[]{:S(2)}) copy-start(bf16[96,1536]{1,0:T(8,128)(2,1)} %param.15) | copy-start | bytes 884740
  7.2 134.3 %all-reduce.3.cloned.1.call-start = ((), (), s32[]{:S(2)}) async-start(), calls=%async_computation | async-start | bytes 1048576 | tf_op jit(solution)/shard_map/psum | solution.py:95
  7.2 10.2 %collective-permute-start = (bf16[96,1536]{1,0:T(8,128)(2,1)}, bf16[96,1536]{1,0:T(8,128)(2,1)S(1)}, u32[]{:S(2)}, u32[]{:S(2)}) collective-permute-start(bf16[96,1536]{1,0:T(8,128)(2,1)} %param.16), channel_id=1, source_target_pairs={{0,1},{1,2},{2,3},{3,4},{4,5},{5,6},{6,7},{7,8},{8,9},{9,10},{10,1... | collective-permute-start | bytes 884744 | tf_op jit(solution)/shard_map/ppermute | solution.py:17
  7.7 19.8 %collective-permute-start.8 = (bf16[96,1536]{1,0:T(8,128)(2,1)}, bf16[96,1536]{1,0:T(8,128)(2,1)S(1)}, u32[]{:S(2)}, u32[]{:S(2)}) collective-permute-start(bf16[96,1536]{1,0:T(8,128)(2,1)} %param.16), channel_id=1, source_target_pairs={{0,15},{1,0},{2,1},{3,2},{4,3},{5,4},{6,5},{7,6},{8,7},{9,8},{10,9... | collective-permute-start | bytes 884744 | tf_op jit(solution)/shard_map/ppermute | solution.py:19
  17.5 8.8 %collective-permute-start.1 = (bf16[96,1536]{1,0:T(8,128)(2,1)S(1)}, bf16[96,1536]{1,0:T(8,128)(2,1)S(1)}, u32[]{:S(2)}, u32[]{:S(2)}) collective-permute-start(bf16[96,1536]{1,0:T(8,128)(2,1)S(1)} %collective-permute-done), channel_id=1, source_target_pairs={{0,1},{1,2},{2,3},{3,4},{4,5},{5,6},{6,7},{7,8},{8,9},{9,10},{10,1... | collective-permute-start | bytes 884744 | tf_op jit(solution)/shard_map/ppermute | solution.py:17
  26.3 17.9 %copy-start.9 = (bf16[96,1536]{1,0:T(8,128)(2,1)}, bf16[96,1536]{1,0:T(8,128)(2,1)S(1)}, u32[]{:S(2)}) copy-start(bf16[96,1536]{1,0:T(8,128)(2,1)S(1)} %collective-permute-done.1) | copy-start | bytes 884740
  26.3 9.0 %collective-permute-start.2 = (bf16[96,1536]{1,0:T(8,128)(2,1)S(1)}, bf16[96,1536]{1,0:T(8,128)(2,1)S(1)}, u32[]{:S(2)}, u32[]{:S(2)}) collective-permute-start(bf16[96,1536]{1,0:T(8,128)(2,1)S(1)} %collective-permute-done.1), channel_id=1, source_target_pairs={{0,1},{1,2},{2,3},{3,4},{4,5},{5,6},{6,7},{7,8},{8,9},{9,10},{10,1... | collective-permute-start | bytes 884744 | tf_op jit(solution)/shard_map/ppermute | solution.py:17
  27.6 8.9 %collective-permute-start.9 = (bf16[96,1536]{1,0:T(8,128)(2,1)S(1)}, bf16[96,1536]{1,0:T(8,128)(2,1)S(1)}, u32[]{:S(2)}, u32[]{:S(2)}) collective-permute-start(bf16[96,1536]{1,0:T(8,128)(2,1)S(1)} %collective-permute-done.8), channel_id=1, source_target_pairs={{0,15},{1,0},{2,1},{3,2},{4,3},{5,4},{6,5},{7,6},{8,7},{9,8},{10,9... | collective-permute-start | bytes 884744 | tf_op jit(solution)/shard_map/ppermute | solution.py:19
  35.3 32.5 %copy-start.13 = (bf16[96,1536]{1,0:T(8,128)(2,1)}, bf16[96,1536]{1,0:T(8,128)(2,1)S(1)}, u32[]{:S(2)}) copy-start(bf16[96,1536]{1,0:T(8,128)(2,1)S(1)} %collective-permute-done.2) | copy-start | bytes 884740
  35.3 9.0 %collective-permute-start.3 = (bf16[96,1536]{1,0:T(8,128)(2,1)S(1)}, bf16[96,1536]{1,0:T(8,128)(2,1)S(1)}, u32[]{:S(2)}, u32[]{:S(2)}) collective-permute-start(bf16[96,1536]{1,0:T(8,128)(2,1)S(1)} %collective-permute-done.2), channel_id=1, source_target_pairs={{0,1},{1,2},{2,3},{3,4},{4,5},{5,6},{6,7},{7,8},{8,9},{9,10},{10,1... | collective-permute-start | bytes 884744 | tf_op jit(solution)/shard_map/ppermute | solution.py:17
  36.4 31.3 %copy-start.11 = (bf16[96,1536]{1,0:T(8,128)(2,1)}, bf16[96,1536]{1,0:T(8,128)(2,1)S(1)}, u32[]{:S(2)}) copy-start(bf16[96,1536]{1,0:T(8,128)(2,1)S(1)} %collective-permute-done.9) | copy-start | bytes 884740
  36.5 16.0 %collective-permute-start.10 = (bf16[96,1536]{1,0:T(8,128)(2,1)S(1)}, bf16[96,1536]{1,0:T(8,128)(2,1)S(1)}, u32[]{:S(2)}, u32[]{:S(2)}) collective-permute-start(bf16[96,1536]{1,0:T(8,128)(2,1)S(1)} %collective-permute-done.9), channel_id=1, source_target_pairs={{0,15},{1,0},{2,1},{3,2},{4,3},{5,4},{6,5},{7,6},{8,7},{9,8},{10,9... | collective-permute-start | bytes 884744 | tf_op jit(solution)/shard_map/ppermute | solution.py:19
  44.2 23.5 %copy-start.17 = (bf16[96,1536]{1,0:T(8,128)(2,1)}, bf16[96,1536]{1,0:T(8,128)(2,1)S(1)}, u32[]{:S(2)}) copy-start(bf16[96,1536]{1,0:T(8,128)(2,1)S(1)} %collective-permute-done.3) | copy-start | bytes 884740
  44.2 12.7 %collective-permute-start.4 = (bf16[96,1536]{1,0:T(8,128)(2,1)S(1)}, bf16[96,1536]{1,0:T(8,128)(2,1)S(1)}, u32[]{:S(2)}, u32[]{:S(2)}) collective-permute-start(bf16[96,1536]{1,0:T(8,128)(2,1)S(1)} %collective-permute-done.3), channel_id=1, source_target_pairs={{0,1},{1,2},{2,3},{3,4},{4,5},{5,6},{6,7},{7,8},{8,9},{9,10},{10,1... | collective-permute-start | bytes 884744 | tf_op jit(solution)/shard_map/ppermute | solution.py:17
  45.7 173.8 %all-gather.3.cloned.1.call-start = ((), (), s32[]{:S(2)}) async-start(), calls=%async_computation.1 | async-start | bytes 5013504 | tf_op jit(solution)/shard_map/all_gather | solution.py:119
  46.4 289.0 %all-reduce.5.cloned.1.call-start = ((), (), s32[]{:S(2)}) async-start(), calls=%async_computation.2 | async-start | bytes 1048576 | tf_op jit(solution)/shard_map/psum | solution.py:46
  52.5 15.3 %copy-start.15 = (bf16[96,1536]{1,0:T(8,128)(2,1)}, bf16[96,1536]{1,0:T(8,128)(2,1)S(1)}, u32[]{:S(2)}) copy-start(bf16[96,1536]{1,0:T(8,128)(2,1)S(1)} %collective-permute-done.10) | copy-start | bytes 884740
  52.5 15.6 %collective-permute-start.11 = (bf16[96,1536]{1,0:T(8,128)(2,1)S(1)}, bf16[96,1536]{1,0:T(8,128)(2,1)S(1)}, u32[]{:S(2)}, u32[]{:S(2)}) collective-permute-start(bf16[96,1536]{1,0:T(8,128)(2,1)S(1)} %collective-permute-done.10), channel_id=1, source_target_pairs={{0,15},{1,0},{2,1},{3,2},{4,3},{5,4},{6,5},{7,6},{8,7},{9,8},{10,9... | collective-permute-start | bytes 884744 | tf_op jit(solution)/shard_map/ppermute | solution.py:19
  56.9 10.8 %copy-start.19 = (bf16[96,1536]{1,0:T(8,128)(2,1)}, bf16[96,1536]{1,0:T(8,128)(2,1)S(1)}, u32[]{:S(2)}) copy-start(bf16[96,1536]{1,0:T(8,128)(2,1)S(1)} %collective-permute-done.4) | copy-start | bytes 884740
  56.9 15.6 %collective-permute-start.5 = (bf16[96,1536]{1,0:T(8,128)(2,1)S(1)}, bf16[96,1536]{1,0:T(8,128)(2,1)S(1)}, u32[]{:S(2)}, u32[]{:S(2)}) collective-permute-start(bf16[96,1536]{1,0:T(8,128)(2,1)S(1)} %collective-permute-done.4), channel_id=1, source_target_pairs={{0,1},{1,2},{2,3},{3,4},{4,5},{5,6},{6,7},{7,8},{8,9},{9,10},{10,1... | collective-permute-start | bytes 884744 | tf_op jit(solution)/shard_map/ppermute | solution.py:17
  68.0 23.7 %copy-start.21 = (bf16[96,1536]{1,0:T(8,128)(2,1)}, bf16[96,1536]{1,0:T(8,128)(2,1)S(1)}, u32[]{:S(2)}) copy-start(bf16[96,1536]{1,0:T(8,128)(2,1)S(1)} %collective-permute-done.11) | copy-start | bytes 884740
  68.0 23.8 %collective-permute-start.12 = (bf16[96,1536]{1,0:T(8,128)(2,1)S(1)}, bf16[96,1536]{1,0:T(8,128)(2,1)}, u32[]{:S(2)}, u32[]{:S(2)}) collective-permute-start(bf16[96,1536]{1,0:T(8,128)(2,1)S(1)} %collective-permute-done.11), channel_id=1, source_target_pairs={{0,15},{1,0},{2,1},{3,2},{4,3},{5,4},{6,5},{7,6},{8,7},{9,8},{10,9... | collective-permute-start | bytes 884744 | tf_op jit(solution)/shard_map/ppermute | solution.py:19
  72.4 19.3 %copy-start.23 = (bf16[96,1536]{1,0:T(8,128)(2,1)}, bf16[96,1536]{1,0:T(8,128)(2,1)S(1)}, u32[]{:S(2)}) copy-start(bf16[96,1536]{1,0:T(8,128)(2,1)S(1)} %collective-permute-done.5) | copy-start | bytes 884740
  72.4 23.8 %collective-permute-start.6 = (bf16[96,1536]{1,0:T(8,128)(2,1)S(1)}, bf16[96,1536]{1,0:T(8,128)(2,1)}, u32[]{:S(2)}, u32[]{:S(2)}) collective-permute-start(bf16[96,1536]{1,0:T(8,128)(2,1)S(1)} %collective-permute-done.5), channel_id=1, source_target_pairs={{0,1},{1,2},{2,3},{3,4},{4,5},{5,6},{6,7},{7,8},{8,9},{9,10},{10,1... | collective-permute-start | bytes 884744 | tf_op jit(solution)/shard_map/ppermute | solution.py:17
  84.1 12.1 %copy-start.26 = (f32[1536]{0:T(1024)S(1)}, f32[1536]{0:T(1024)}, u32[]{:S(2)}) copy-start(f32[1536]{0:T(1024)} %param.12) | copy-start | bytes 18436
  84.4 28.0 %copy-start.8 = (bf16[96,1536]{1,0:T(8,128)(2,1)S(1)}, bf16[96,1536]{1,0:T(8,128)(2,1)}, u32[]{:S(2)}) copy-start(bf16[96,1536]{1,0:T(8,128)(2,1)} %param.16) | copy-start | bytes 884740
  91.9 8.9 %collective-permute-start.13 = (bf16[96,1536]{1,0:T(8,128)(2,1)}, bf16[96,1536]{1,0:T(8,128)(2,1)}, u32[]{:S(2)}, u32[]{:S(2)}) collective-permute-start(bf16[96,1536]{1,0:T(8,128)(2,1)} %collective-permute-done.12), channel_id=1, source_target_pairs={{0,15},{1,0},{2,1},{3,2},{4,3},{5,4},{6,5},{7,6},{8,7},{9,8},{10,9... | collective-permute-start | bytes 884744 | tf_op jit(solution)/shard_map/ppermute | solution.py:19
  96.2 9.3 %collective-permute-start.7 = (bf16[96,1536]{1,0:T(8,128)(2,1)}, bf16[96,1536]{1,0:T(8,128)(2,1)}, u32[]{:S(2)}, u32[]{:S(2)}) collective-permute-start(bf16[96,1536]{1,0:T(8,128)(2,1)} %collective-permute-done.6), channel_id=1, source_target_pairs={{0,1},{1,2},{2,3},{3,4},{4,5},{5,6},{6,7},{7,8},{8,9},{9,10},{10,1... | collective-permute-start | bytes 884744 | tf_op jit(solution)/shard_map/ppermute | solution.py:17
  99.3 20.2 %copy-start.24 = (bf16[96,1536]{1,0:T(8,128)(2,1)S(1)}, bf16[96,1536]{1,0:T(8,128)(2,1)}, u32[]{:S(2)}) copy-start(bf16[96,1536]{1,0:T(8,128)(2,1)} %copy-done.23) | copy-start | bytes 884740
  99.4 20.2 %copy-start.20 = (bf16[96,1536]{1,0:T(8,128)(2,1)S(1)}, bf16[96,1536]{1,0:T(8,128)(2,1)}, u32[]{:S(2)}) copy-start(bf16[96,1536]{1,0:T(8,128)(2,1)} %copy-done.19) | copy-start | bytes 884740
  99.4 20.2 %copy-start.18 = (bf16[96,1536]{1,0:T(8,128)(2,1)S(1)}, bf16[96,1536]{1,0:T(8,128)(2,1)}, u32[]{:S(2)}) copy-start(bf16[96,1536]{1,0:T(8,128)(2,1)} %copy-done.17) | copy-start | bytes 884740
  99.4 20.2 %copy-start.14 = (bf16[96,1536]{1,0:T(8,128)(2,1)S(1)}, bf16[96,1536]{1,0:T(8,128)(2,1)}, u32[]{:S(2)}) copy-start(bf16[96,1536]{1,0:T(8,128)(2,1)} %copy-done.13) | copy-start | bytes 884740
  99.4 20.3 %copy-start.10 = (bf16[96,1536]{1,0:T(8,128)(2,1)S(1)}, bf16[96,1536]{1,0:T(8,128)(2,1)}, u32[]{:S(2)}) copy-start(bf16[96,1536]{1,0:T(8,128)(2,1)} %copy-done.9) | copy-start | bytes 884740
  99.4 20.4 %copy-start.12 = (bf16[96,1536]{1,0:T(8,128)(2,1)S(1)}, bf16[96,1536]{1,0:T(8,128)(2,1)}, u32[]{:S(2)}) copy-start(bf16[96,1536]{1,0:T(8,128)(2,1)} %copy-done.11) | copy-start | bytes 884740
  99.4 20.4 %copy-start.16 = (bf16[96,1536]{1,0:T(8,128)(2,1)S(1)}, bf16[96,1536]{1,0:T(8,128)(2,1)}, u32[]{:S(2)}) copy-start(bf16[96,1536]{1,0:T(8,128)(2,1)} %copy-done.15) | copy-start | bytes 884740
  99.4 20.5 %copy-start.22 = (bf16[96,1536]{1,0:T(8,128)(2,1)S(1)}, bf16[96,1536]{1,0:T(8,128)(2,1)}, u32[]{:S(2)}) copy-start(bf16[96,1536]{1,0:T(8,128)(2,1)} %copy-done.21) | copy-start | bytes 884740
  100.8 16.7 %collective-permute-start.14 = (bf16[96,1536]{1,0:T(8,128)(2,1)}, bf16[96,1536]{1,0:T(8,128)(2,1)S(1)}, u32[]{:S(2)}, u32[]{:S(2)}) collective-permute-start(bf16[96,1536]{1,0:T(8,128)(2,1)} %collective-permute-done.13), channel_id=1, source_target_pairs={{0,15},{1,0},{2,1},{3,2},{4,3},{5,4},{6,5},{7,6},{8,7},{9,8},{10,9... | collective-permute-start | bytes 884744 | tf_op jit(solution)/shard_map/ppermute | solution.py:19
  141.4 74.9 %copy-start.4 = (f32[64,16,96]{2,0,1:T(8,128)S(1)}, f32[64,16,96]{2,0,1:T(8,128)}, u32[]{:S(2)}) copy-start(f32[64,16,96]{2,0,1:T(8,128)} %all-reduce.3.cloned.1.call-done) | copy-start | bytes 1179652
  218.5 0.8 copy-start.5
  225.6 2.4 copy-start.2
  230.6 17.4 %slice-start = ((f32[864,1536]{1,0:T(8,128)}), f32[64,1536]{1,0:T(8,128)S(1)}, s32[]{:S(2)}) async-start(f32[864,1536]{1,0:T(8,128)} %copy-done.2), calls=%async_computation.3 | async-start | bytes 786432 | tf_op jit(solution)/shard_map/slice | solution.py:129
  230.6 104.8 %copy-start.6 = (f32[16,64,64]{1,2,0:T(8,128)S(1)}, f32[16,64,64]{1,2,0:T(8,128)}, u32[]{:S(2)}) copy-start(f32[16,64,64]{1,2,0:T(8,128)} %copy-done.5) | copy-start | bytes 786436
  236.7 101.6 %copy-start.25 = (bf16[1536,96]{0,1:T(8,128)(2,1)S(1)}, bf16[1536,96]{0,1:T(8,128)(2,1)}, u32[]{:S(2)}) copy-start(bf16[1536,96]{0,1:T(8,128)(2,1)} %param.18) | copy-start | bytes 884740
  236.7 124.7 %copy-start.3 = (bf16[64,1536]{1,0:T(8,128)(2,1)S(1)}, bf16[64,1536]{1,0:T(8,128)(2,1)}, u32[]{:S(2)}) copy-start(bf16[64,1536]{1,0:T(8,128)(2,1)} %param.13) | copy-start | bytes 589828
  236.7 125.5 %copy-start.1 = (bf16[96,1536]{1,0:T(8,128)(2,1)S(1)}, bf16[96,1536]{1,0:T(8,128)(2,1)}, u32[]{:S(2)}) copy-start(bf16[96,1536]{1,0:T(8,128)(2,1)} %param.15) | copy-start | bytes 884740
  361.4 0.8 copy-start.7
Sparse Core Ops, SparseCore 0:
  45.8 95.6 all-reduce.2
  143.7 54.5 all-gather.2
  248.1 87.2 all-reduce.4
